TPU v7x, 32 devices: a whole 2x2x4 slice. The times are simulated.
32 devices in a mesh: walk: 8 (over z, x), pt: 4 (over y, core).
Axes of the slice: x: 2, y: 2, z: 4, core: 2. Of those that a mesh axis runs over, the one named last changes fastest.
Arguments:
- bra_orbitals: bfloat16 [8, 1536, 160], P('walk'), may hold values from -6 to 6
- ket_orbitals: bfloat16 [8, 1536, 160], P('walk'), may hold values from -6 to 6
- collocation: bfloat16 [12288, 1536], P('pt'), may hold values from -0.15625 to 0.15625
- kernel: bfloat16 [12288, 12288], P('pt', 'walk'), as said below
- walker_weight: float32 [8], P('walk'), may hold values from 0.3 to 3
- walker_group: int32 [8], P('walk'), may hold values from 0 to 19
- group_occupied: int32 [20], replicated, may hold values from 80 to 160, as said below
Outputs:
- gradient: float32 [12288, 1536], P('pt', 'walk')
Inputs may be any that keep to these rules, and one draw needn't show every extreme that they name: kernel is symmetric. `group_occupied`: some group has exactly 160 occupied orbitals.
All inputs are finite; a program needn't handle non-finite values.
Results may differ from a plain program's by a relative error of at most 0.0064.
Values may be sent and summed in bfloat16 or wider, within the bound.
No kernel may reach another device: no remote copies, remote signals or barrier semaphores. Data moves between devices by JAX's collectives and lax.ppermute only.
A program may use at most 192 MiB of HBM per device.

v0:
```python
import jax
import jax.numpy as jnp
from jax import lax
from jax.sharding import PartitionSpec as P


def on_device(
    bra_orbitals, ket_orbitals, collocation, kernel, walker_weight, walker_group, group_occupied
):
    group_count = group_occupied.shape[0]
    occ_width = bra_orbitals.shape[2]
    matches = walker_group[:, None] == jnp.arange(group_count, dtype=jnp.int32)[None, :]
    occupied = jnp.sum(jnp.where(matches, group_occupied[None, :], 0), axis=1)
    masks = (jnp.arange(occ_width, dtype=jnp.int32)[None, :] < occupied[:, None]).astype(
        jnp.bfloat16
    )
    left_bra = bra_orbitals * masks[:, None, :]
    right_ket = ket_orbitals * masks[:, None, :]
    lefts = jnp.einsum(
        "pm,wmk->wpk", collocation, left_bra, preferred_element_type=jnp.float32
    ).astype(jnp.bfloat16)
    rights = jnp.einsum(
        "pm,wmk->wpk", collocation, right_ket, preferred_element_type=jnp.float32
    ).astype(jnp.bfloat16)
    weight_sum = lax.psum(jnp.sum(walker_weight), "walk")
    factors = walker_weight / weight_sum
    left_all, right_all = (
        lax.all_gather(lefts, "pt", axis=1, tiled=True),
        lax.all_gather(rights, "pt", axis=1, tiled=True),
    )
    kernel_block = lax.all_gather(kernel, "walk", axis=1, tiled=True).astype(jnp.float32)[
        None, :, :
    ]
    green_t = jnp.einsum("wpk,wqk->wpq", rights, left_all, preferred_element_type=jnp.float32)
    green = jnp.einsum("wpk,wqk->wpq", lefts, right_all, preferred_element_type=jnp.float32)
    hadamard_t = (kernel_block * green_t).astype(jnp.bfloat16)
    hadamard = (kernel_block * green).astype(jnp.bfloat16)
    more_left = jnp.einsum(
        "wpq,wqk->wpk", hadamard_t, right_all, preferred_element_type=jnp.float32
    )
    more_right = jnp.einsum("wpq,wqk->wpk", hadamard, left_all, preferred_element_type=jnp.float32)
    grad_left = (2.0 * more_left).astype(jnp.bfloat16)
    grad_right = (2.0 * more_right).astype(jnp.bfloat16)
    terms = jnp.einsum(
        "wpk,wmk->wpm", grad_left, left_bra, preferred_element_type=jnp.float32
    ) + jnp.einsum("wpk,wmk->wpm", grad_right, right_ket, preferred_element_type=jnp.float32)
    partial_sum = jnp.sum(factors[:, None, None] * terms, axis=0)
    result = lax.psum_scatter(partial_sum, "walk", scatter_dimension=1, tiled=True)
    return result


def solution(mesh):
    in_specs = (
        P("walk", None, None),
        P("walk", None, None),
        P("pt", None),
        P("pt", "walk"),
        P("walk"),
        P("walk"),
        P(),
    )
    out_specs = P("pt", "walk")
    return jax.shard_map(
        on_device, mesh=mesh, in_specs=in_specs, out_specs=out_specs, check_vma=False
    )
```

profile of v0, /device:TPU:1, one launch (start us, length us, event | category | flops | bytes accessed | tf_op | source)
XLA Modules:
  0.0 1952.3 jit_solution(5686290011231751796)
XLA Ops:
  6.5 0.0 copy-start.3
  6.5 0.0 all-gather.6.cloned.1.call-start
  7.2 1.3 fusion.47
  8.5 0.6 compare_convert_fusion
  9.1 8.1 convolution_convert_fusion
  17.2 0.0 all-gather.6.cloned.1.call-update
  17.2 0.0 all-gather.8.cloned.1.call-start
  17.2 0.0 copy-done.3
  17.3 7.9 convolution_convert_fusion.1
  25.1 0.0 copy-start.1
  25.1 0.0 all-gather.8.cloned.1.call-update
  25.1 0.0 all-gather.4.cloned.1.call-start
  25.2 0.7 all-gather.4.cloned.1.call-update
  25.9 0.0 reduce-scatter.2.cloned.1.call-start
  25.9 19.6 %psum.7 = f32[1]{0:T(128)} all-reduce(f32[1]{0:T(128)} %param.11), channel_id=1, replica_groups=mesh['walk'=8,'pt'=4] {'walk'}, use_global_device_ids=true, to_apply=%region_0.1 | all-reduce | flops 1 | bytes 8 | tf_op jit(solution)/shard_map/psum | solution.py:25
  46.9 0.0 copy-start.2
  46.9 6.0 all-gather.6.cloned.1.call-done
  52.9 34.6 %all-gather.8.cloned.1.call-done = bf16[1,12288,160]{1,2,0:T(8,128)(2,1)} async-done(((bf16[1,3072,160]{1,2,0:T(8,128)(2,1)}), bf16[1,12288,160]{1,2,0:T(8,128)(2,1)}) %all-gather.8.cloned.1.call-update) | async-done | bytes 3932176 | tf_op jit(solution)/shard_map/all_gather | solution.py:29
  87.4 1425.4 %all-gather.4.cloned.1.call-done = bf16[3072,12288]{1,0:T(8,128)(2,1)} async-done(((bf16[3072,1536]{1,0:T(8,128)(2,1)}), bf16[3072,12288]{1,0:T(8,128)(2,1)}) %all-gather.4.cloned.1.call-update) | async-done | bytes 75497488 | tf_op jit(solution)/shard_map/all_gather | solution.py:31
  1512.8 0.0 copy-done.1
  1512.8 49.8 %fusion.25 = bf16[3072,160]{0,1:T(8,128)(2,1)S(1)} fusion(bf16[1,12288,160]{1,2,0:T(8,128)(2,1)} %all-gather.8.cloned.1.call-done, bf16[3072,12288]{1,0:T(8,128)(2,1)} %all-gather.4.cloned.1.call-done, bf16[1,12288,160]{1,2,0:T(8,128)(2,1)} %all-gather.6.cloned.1.call-done, bf16[160,3072]{1,0:T(8,128)(2,1)S(1)} %copy-done.1), kind=kOutput, calls=%fused_computation.16 | convolution fusion | flops 24273420288 | bytes 85327872 | tf_op jit(solution)/shard_map/wpq,wqk->wpk/dot_general | solution.py:38
  1562.6 0.0 copy-done.2
  1562.6 0.0 copy-start
  1562.6 8.0 fusion.34
  1570.7 0.0 copy-done
  1570.7 49.8 %fusion.20 = bf16[3072,160]{0,1:T(8,128)(2,1)S(1)} fusion(bf16[1,12288,160]{1,2,0:T(8,128)(2,1)} %all-gather.6.cloned.1.call-done, bf16[3072,12288]{1,0:T(8,128)(2,1)} %all-gather.4.cloned.1.call-done, bf16[1,12288,160]{1,2,0:T(8,128)(2,1)} %all-gather.8.cloned.1.call-done, bf16[160,3072]{1,0:T(8,128)(2,1)S(1)} %copy-done), kind=kOutput, calls=%fused_computation.15 | convolution fusion | flops 24273420288 | bytes 85327872 | tf_op jit(solution)/shard_map/wpq,wqk->wpk/dot_general | solution.py:41
  1620.4 11.8 add_multiply_fusion
  1632.3 0.0 reduce-scatter.2.cloned.1.call-update
  1632.3 313.4 %reduce-scatter.2.cloned.1.call-done = f32[3072,192]{0,1:T(8,128)} async-done(((f32[3072,1536]{0,1:T(8,128)}), f32[3072,192]{0,1:T(8,128)}) %reduce-scatter.2.cloned.1.call-update) | async-done | bytes 2359312 | tf_op jit(solution)/shard_map/reduce_scatter | solution.py:48
Async XLA Ops:
  6.5 10.7 copy-start.3
  6.5 46.3 %all-gather.6.cloned.1.call-start = ((), (), s32[]{:S(2)}) async-start(), calls=%async_computation.2 | async-start | bytes 4915200 | tf_op jit(solution)/shard_map/all_gather | solution.py:28
  17.2 70.2 %all-gather.8.cloned.1.call-start = ((), (), s32[]{:S(2)}) async-start(), calls=%async_computation.3 | async-start | bytes 4915200 | tf_op jit(solution)/shard_map/all_gather | solution.py:29
  25.1 1487.7 %copy-start.1 = (bf16[160,3072]{1,0:T(8,128)(2,1)S(1)}, bf16[160,3072]{1,0:T(8,128)(2,1)}, u32[]{:S(2)}) copy-start(bf16[160,3072]{1,0:T(8,128)(2,1)} %convolution_convert_fusion.1) | copy-start | bytes 2949124
  25.1 1487.7 %all-gather.4.cloned.1.call-start = ((), (), s32[]{:S(2)}) async-start(), calls=%async_computation.1 | async-start | bytes 84934656 | tf_op jit(solution)/shard_map/all_gather | solution.py:31
  25.9 1919.8 %reduce-scatter.2.cloned.1.call-start = ((), (), s32[]{:S(2)}) async-start(), calls=%async_computation.4 | async-start | bytes 21233664 | tf_op jit(solution)/shard_map/reduce_scatter | solution.py:48
  46.9 1515.7 %copy-start.2 = (bf16[1,1536,160]{1,2,0:T(8,128)(2,1)S(1)}, bf16[1,1536,160]{1,2,0:T(8,128)(2,1)}, u32[]{:S(2)}) copy-start(bf16[1,1536,160]{1,2,0:T(8,128)(2,1)} %param.7) | copy-start | bytes 1474564
  1562.6 8.1 copy-start
Sparse Core Ops, SparseCore 0:
  17.3 35.4 all-gather.5
  54.4 32.9 all-gather.7
  89.0 1423.7 all-gather.3
  1632.4 313.2 reduce-scatter.1
where the time goes:
time: 1950 us
  waiting for transfers between devices  1780 us (91%)
  matrix products  135 us (7%)
  blocking collectives  19.6 us (1%)
    all_gather x1, waiting for transfers between devices, on_device(): lax.all_gather(kernel, 'walk', axis=1, tiled=True).astype(jnp.float32)  1430 us
    reduce_scatter x1, waiting for transfers between devices, on_device(): lax.psum_scatter(partial_sum, 'walk', scatter_dimension=1, tiled=True)  313 us
    dot_general x1, matrix products, on_device(): jnp.einsum('wpq,wqk->wpk', hadamard_t, right_all, preferred_element_type=...  49.8 us
    dot_general x1, matrix products, on_device(): jnp.einsum('wpq,wqk->wpk', hadamard, left_all, preferred_element_type=jnp...  49.8 us
  transfers between devices with their start and end apart: 4, of which 4 were waited for; matrix products, arithmetic and copies ran while one was open for 0% of the time, Pallas kernels for 0%

commit v1 on v0

v1 whole, which is shorter than its diff:
```python
import functools

import jax
import jax.numpy as jnp
from jax import lax
from jax.experimental import pallas as pl
from jax.experimental.pallas import tpu as pltpu
from jax.sharding import PartitionSpec as P

F32 = jnp.float32
BF16 = jnp.bfloat16
BOTH = ("walk", "pt")


def largest_tile(size, limit):
    tile = limit
    while size % tile:
        tile //= 2
    return tile


def pair_kernel(tile_b, share_ref, kt_ref, lrp_ref, lrq_ref, out_ref):
    occ = lrp_ref.shape[0] // 2
    rows, size_b = kt_ref.shape[0], lrp_ref.shape[1]
    tile_a = lrq_ref.shape[1]
    scale = 2.0 * share_ref[pl.program_id(0)]
    begin = pl.multiple_of(pl.program_id(1) * tile_a, tile_a)
    left_a = lrq_ref[:occ, :].T
    right_a = lrq_ref[occ:, :].T
    nt = (((1,), (1,)), ((), ()))
    total_l = jnp.zeros((tile_a, occ), F32)
    total_r = jnp.zeros((tile_a, occ), F32)
    for at in range(0, size_b, tile_b):
        left_t = lrp_ref[:occ, at : at + tile_b]
        right_t = lrp_ref[occ:, at : at + tile_b]
        kern = kt_ref[pl.ds(begin, tile_a), at : at + tile_b].astype(F32)
        green_t = jnp.dot(right_a, left_t, preferred_element_type=F32)
        had_t = (kern * green_t).astype(BF16)
        green = jnp.dot(left_a, right_t, preferred_element_type=F32)
        had = (kern * green).astype(BF16)
        total_l += lax.dot_general(had_t, right_t, nt, preferred_element_type=F32)
        total_r += lax.dot_general(had, left_t, nt, preferred_element_type=F32)
    out_ref[:occ, :] = (total_l * scale).astype(BF16).T
    out_ref[occ:, :] = (total_r * scale).astype(BF16).T


def pair_gradients(share, kernel_t, lrp, lrq, walkers):
    size_a, size_b = kernel_t.shape
    width = lrp.shape[0] // walkers
    tile_a = largest_tile(size_a, 512)
    tile_b = largest_tile(size_b, 512)
    return pl.pallas_call(
        functools.partial(pair_kernel, tile_b),
        out_shape=jax.ShapeDtypeStruct((lrp.shape[0], size_a), BF16),
        grid_spec=pltpu.PrefetchScalarGridSpec(
            num_scalar_prefetch=1,
            grid=(walkers, size_a // tile_a),
            in_specs=[
                pl.BlockSpec((size_a, size_b), lambda w, a, s: (0, 0), pipeline_mode=pl.Buffered(1)),
                pl.BlockSpec((width, size_b), lambda w, a, s: (w, 0)),
                pl.BlockSpec((width, tile_a), lambda w, a, s: (w, a)),
            ],
            out_specs=pl.BlockSpec((width, tile_a), lambda w, a, s: (w, a)),
        ),
        compiler_params=pltpu.CompilerParams(vmem_limit_bytes=56 * 1024 * 1024),
        cost_estimate=pl.CostEstimate(
            flops=2 * 4 * lrp.shape[0] // 2 * size_a * size_b,
            bytes_accessed=2 * (size_a * size_b + 2 * lrp.size + 2 * lrq.size),
            transcendentals=0,
        ),
    )(share, kernel_t, lrp, lrq)


def send(x, axes, pairs):
    return lax.ppermute(x, axes, pairs)


def gather_ring(own, count):
    z_size = count // 2
    walk = range(count)
    mine = [own]
    for r in range(1, z_size):
        mine.append(send(own, "walk", [(j, (j - 2 * r) % count) for j in walk]))
    across = [send(part, "walk", [(j, j ^ 1) for j in walk]) for part in mine]
    slots = []
    for part in [p for pair in zip(mine, across) for p in pair]:
        other = send(part, "pt", [(i, i ^ 1) for i in range(4)])
        slots += [part, other]
    return jnp.concatenate(slots, axis=0)


def on_device(nw, npt, bra_orbitals, ket_orbitals, collocation, kernel, walker_weight, walker_group, group_occupied):
    group_count = group_occupied.shape[0]
    local, size_m, occ = bra_orbitals.shape
    walkers = nw * local
    size_b, size_a = kernel.shape
    me_w, me_p = lax.axis_index("walk"), lax.axis_index("pt")
    fast = nw == 8 and npt == 4 and local == 1 and size_b == 2 * size_a and size_m % nw == 0

    matches = walker_group[:, None] == jnp.arange(group_count, dtype=jnp.int32)[None, :]
    occupied = jnp.sum(jnp.where(matches, group_occupied[None, :], 0), axis=1)
    masks = (jnp.arange(occ, dtype=jnp.int32)[None, :] < occupied[:, None]).astype(BF16)
    bra_t = jnp.swapaxes(bra_orbitals * masks[:, None, :], 1, 2)
    ket_t = jnp.swapaxes(ket_orbitals * masks[:, None, :], 1, 2)
    weights = lax.all_gather(walker_weight, "walk", axis=0, tiled=True)
    shares = weights / jnp.sum(weights)
    kernel_t = kernel.T

    if fast:
        parity = me_p % 2
        own = jnp.where(parity == 0, bra_t[0], ket_t[0])
        orbitals = gather_ring(own, nw)
        slot = jnp.arange(walkers, dtype=jnp.int32)
        shares = shares[((me_w // 2 + slot // 2) % (nw // 2)) * 2 + (me_w + slot) % 2]
        z = me_w // 2
        rows = lax.dynamic_slice_in_dim(collocation, (me_w % 2) * size_a, size_a, 0)
        far = send(rows, BOTH, [(j * npt + j // 2, j * npt + (j // 2 ^ 2)) for j in range(nw)])
        near = jnp.where(me_p == z, rows, far)
        swap = [(j * npt + (j // 2 ^ s), j * npt + (j // 2 ^ s ^ 1)) for j in range(nw) for s in (0, 2)]
        col_q = jnp.where(parity == z % 2, near, send(near, BOTH, swap))
    else:
        both = jnp.concatenate([bra_t, ket_t], axis=1).reshape(local * 2 * occ, size_m)
        orbitals = lax.all_gather(both, "walk", axis=0, tiled=True)
        owner = (me_w * size_a) // size_b
        all_rows = lax.all_gather(collocation, "pt", axis=0, tiled=True)
        col_q = lax.dynamic_slice_in_dim(all_rows, me_w * size_a, size_a, 0)

    nt = (((1,), (1,)), ((), ()))
    lrp = lax.dot_general(orbitals, collocation, nt, preferred_element_type=F32).astype(BF16)
    lrq = lax.dot_general(orbitals, col_q, nt, preferred_element_type=F32).astype(BF16)
    grads = pair_gradients(shares, kernel_t, lrp, lrq, walkers)
    tn = (((0,), (0,)), ((), ()))
    part = lax.dot_general(orbitals, grads, tn, preferred_element_type=F32)

    if fast:
        half, quarter, eighth = size_m // 2, size_m // 4, size_m // 8
        y = me_p // 2
        part = part.astype(BF16)
        give = lax.dynamic_slice_in_dim(part, (1 - parity) * half, half, 0)
        keep = lax.dynamic_slice_in_dim(part, parity * half, half, 0)
        got = send(give, "pt", [(i, i ^ 1) for i in range(npt)])
        part = (keep.astype(F32) + got.astype(F32)).astype(BF16)
        give = lax.dynamic_slice_in_dim(part, (1 - y) * quarter, quarter, 0)
        keep = lax.dynamic_slice_in_dim(part, y * quarter, quarter, 0)
        got = send(give, "pt", [(i, i ^ 2) for i in range(npt)])
        part = (keep.astype(F32) + got.astype(F32)).astype(BF16)
        x = me_w % 2
        landed = []
        for t in (0, 1):
            piece = lax.dynamic_slice_in_dim(part, (x ^ t) * eighth, eighth, 0)
            pairs = []
            for j in range(nw):
                for i in range(npt):
                    quarter_of = 2 * (i % 2) + i // 2
                    pairs.append((j * npt + i, (2 * quarter_of + (j % 2 ^ t)) * npt + j // 2))
            landed.append(send(piece, BOTH, pairs))
        first = jnp.where(x == 0, landed[0], landed[1])
        second = jnp.where(x == 0, landed[1], landed[0])
        return jnp.concatenate([first, second], axis=1).astype(F32).T
    part = lax.psum(part, "pt")
    part = jnp.where(owner == me_p, part, 0.0)
    wide = jnp.zeros((size_m, size_b), F32)
    wide = lax.dynamic_update_slice_in_dim(wide, part, (me_w * size_a) % size_b, 1)
    return lax.psum_scatter(wide, "walk", scatter_dimension=0, tiled=True).T


def solution(mesh):
    in_specs = (
        P("walk", None, None),
        P("walk", None, None),
        P("pt", None),
        P("pt", "walk"),
        P("walk"),
        P("walk"),
        P(),
    )
    out_specs = P("pt", "walk")
    body = functools.partial(on_device, mesh.shape["walk"], mesh.shape["pt"])
    return jax.shard_map(body, mesh=mesh, in_specs=in_specs, out_specs=out_specs, check_vma=False)
```

time: 1950 us -> 358 us (0.18)
  waiting for transfers between devices: 1780 us -> 82.8 us
  Pallas kernels: 0 us -> 92 us
  matrix products: 135 us -> 61.6 us
  starting transfers between devices: 0.12 us -> 38 us
  local copies, waits for them, and re-layouts: 0.02 us -> 36 us
    all_gather x3 -> x0, waiting for transfers between devices: 1470 us -> none  [the longest x1 1430 us: on_device(): lax.all_gather(kernel, 'walk', axis=1, tiled=True).astype(jnp.float32)]
    reduce_scatter x1 -> x0, waiting for transfers between devices: 313 us -> none  [on_device(): lax.psum_scatter(partial_sum, 'walk', scatter_dimension=1, tiled=True)]
    pallas_call x0 -> x1, Pallas kernels: none -> 92 us  [pair_gradients(): pl.pallas_call(functools.partial(pair_kernel, tile_b), out_shape=jax.Shap...]
    ppermute x0 -> x21, waiting for transfers between devices: none -> 82.8 us  [send(): return lax.ppermute(x, axes, pairs)]
    dot_general x6 -> x3, matrix products: 135 us -> 61.6 us  [the longest x1 28.4 us: on_device(): lax.dot_general(orbitals, collocation, nt, preferred_element_type=F32)]
    ppermute x0 -> x21, starting transfers between devices: none -> 38 us  [send(): return lax.ppermute(x, axes, pairs)]
    unnamed x0 -> x1, blocking collectives: none -> 30.2 us
    unnamed x8 -> x38, local copies, waits for them, and re-layouts: 0.02 us -> 28.8 us
  transfers between devices with their start and end apart: 4 -> 21, of which waited for: 4 -> 6; matrix products, arithmetic and copies ran while one was open for 0% -> 18% of each run, Pallas kernels for 0% -> 0%
where the time goes in v1:
time: 358 us; the launch traced here: 357 us
  Pallas kernels  92 us (26%)
  waiting for transfers between devices  82.8 us (23%)
  matrix products  61.6 us (17%)
  starting transfers between devices  38 us (11%)
  local copies, waits for them, and re-layouts  36 us (10%)
  blocking collectives  30.2 us (8%)
  other arithmetic  15.1 us (4%)
    pallas_call x1, Pallas kernels, pair_gradients(): pl.pallas_call(functools.partial(pair_kernel, tile_b), out_shape=jax.Shap...  92 us
    ppermute x21, waiting for transfers between devices, send(): return lax.ppermute(x, axes, pairs)  82.8 us
    ppermute x21, starting transfers between devices, send(): return lax.ppermute(x, axes, pairs)  38 us
    unnamed x1, blocking collectives  30.2 us
    unnamed x38, local copies, waits for them, and re-layouts  28.8 us
    dot_general x1, matrix products, on_device(): lax.dot_general(orbitals, collocation, nt, preferred_element_type=F32)  28.4 us
    dot_general x1, matrix products, on_device(): lax.dot_general(orbitals, col_q, nt, preferred_element_type=F32)  18.2 us
    dot_general x1, matrix products, on_device(): part = lax.dot_general(orbitals, grads, tn, preferred_element_type=F32)  14.9 us
  transfers between devices with their start and end apart: 21, of which 6 were waited for; matrix products, arithmetic and copies ran while one was open for 18% of the time, Pallas kernels for 0%

profile of v1, /device:TPU:1, one launch (start us, length us, event | category | flops | bytes accessed | tf_op | source)
XLA Modules:
  0.0 357.2 jit_solution(3777451066883569132)
XLA Ops:
  0.0 4.9 %constant_dynamic-slice_fusion.4 = bf16[1536,1536]{1,0:T(8,128)(2,1)} fusion(bf16[3072,1536]{1,0:T(8,128)(2,1)} %param.9, s32[]{:T(128)S(6)} %select_n.153), kind=kLoop, calls=%fused_computation.44 | loop fusion | bytes 9437188 | tf_op jit(solution)/shard_map/dynamic_slice | solution.py:116
  4.9 2.8 collective-permute-start.15
  8.4 0.7 fusion.4
  9.1 0.6 compare_convert_fusion
  9.8 1.0 constant_dynamic-update-slice_fusion.15
  10.8 4.3 %collective-permute-start = (bf16[160,1536]{1,0:T(8,128)(2,1)S(1)}, bf16[160,1536]{1,0:T(8,128)(2,1)S(1)}, u32[]{:S(2)}, u32[]{:S(2)}) collective-permute-start(bf16[160,1536]{1,0:T(8,128)(2,1)S(1)} %get-tuple-element.6), channel_id=1, source_target_pairs={{0,1},{1,0},{2,3},{3,2},{4,5},{5,4},{6,7},{7,6},{8,9},{9,8},{10,11... | collective-permute-start | bytes 1474568 | tf_op jit(solution)/shard_map/ppermute | solution.py:75
  15.1 1.2 collective-permute-start.1
  16.3 0.6 collective-permute-start.3
  17.5 0.6 dynamic-slice
  18.1 0.8 dynamic-update-slice
  18.8 1.0 collective-permute-start.7
  19.8 30.2 %all-reduce = f32[8]{0:T(128)S(1)} all-reduce(f32[8]{0:T(128)S(1)} %dynamic-update-slice), channel_id=1, replica_groups=mesh['walk'=8,'pt'=4] {'walk'}, use_global_device_ids=true, to_apply=%add | all-reduce | flops 8 | bytes 64
  50.0 0.6 reduce_sum.19
  50.6 0.6 broadcast_divide_fusion
  51.3 6.1 %collective-permute-start.11 = (bf16[160,1536]{1,0:T(8,128)(2,1)S(1)}, bf16[160,1536]{1,0:T(8,128)(2,1)S(1)}, u32[]{:S(2)}, u32[]{:S(2)}) collective-permute-start(bf16[160,1536]{1,0:T(8,128)(2,1)S(1)} %get-tuple-element.6), channel_id=1, source_target_pairs={{0,8},{4,12},{8,16},{12,20},{16,24},{20,28},{24,0},{28,4},{1,9},{5... | collective-permute-start | bytes 1474568 | tf_op jit(solution)/shard_map/ppermute | solution.py:75
  57.4 4.9 %collective-permute-start.2 = (bf16[160,1536]{1,0:T(8,128)(2,1)S(1)}, bf16[160,1536]{1,0:T(8,128)(2,1)}, u32[]{:S(2)}, u32[]{:S(2)}) collective-permute-start(bf16[160,1536]{1,0:T(8,128)(2,1)S(1)} %collective-permute-done.1), channel_id=1, source_target_pairs={{0,1},{1,0},{2,3},{3,2},{4,5},{5,4},{6,7},{7,6},{8,9},{9,8},{10,11... | collective-permute-start | bytes 1474568 | tf_op jit(solution)/shard_map/ppermute | solution.py:75
  62.2 0.5 collective-permute-start.5
  62.8 12.7 %copy.9 = bf16[3072,1536]{0,1:T(8,128)(2,1)} copy(bf16[3072,1536]{1,0:T(8,128)(2,1)} %param.10) | data formatting | bytes 18874368 | tf_op args[3]
  75.5 1.2 gather_fusion
  76.6 0.8 constant_dynamic-update-slice_fusion.14
  77.5 0.3 collective-permute-start.4
  77.8 0.8 constant_dynamic-update-slice_fusion.13
  78.6 1.0 collective-permute-start.9
  79.6 0.5 collective-permute-start.13
  80.1 0.7 collective-permute-start.6
  80.8 1.9 constant_dynamic-update-slice_fusion.12
  82.7 0.8 constant_dynamic-update-slice_fusion.11
  83.5 0.8 constant_dynamic-update-slice_fusion.10
  84.4 0.8 constant_dynamic-update-slice_fusion.9
  85.2 6.1 %collective-permute-done.9 = bf16[160,1536]{1,0:T(8,128)(2,1)S(1)} collective-permute-done((bf16[160,1536]{1,0:T(8,128)(2,1)S(1)}, bf16[160,1536]{1,0:T(8,128)(2,1)S(1)}, u32[]{:S(2)}, u32[]{:S(2)}) %collective-permute-start.9) | collective-permute-done | bytes 491552 | tf_op jit(solution)/shard_map/ppermute | solution.py:75
  91.3 1.5 collective-permute-start.12
  92.8 9.0 %collective-permute-done.13 = bf16[160,1536]{1,0:T(8,128)(2,1)S(1)} collective-permute-done((bf16[160,1536]{1,0:T(8,128)(2,1)S(1)}, bf16[160,1536]{1,0:T(8,128)(2,1)S(1)}, u32[]{:S(2)}, u32[]{:S(2)}) %collective-permute-start.13) | collective-permute-done | bytes 491552 | tf_op jit(solution)/shard_map/ppermute | solution.py:75
  101.8 1.0 collective-permute-start.10
  102.8 0.8 constant_dynamic-update-slice_fusion.8
  103.6 0.8 constant_dynamic-update-slice_fusion.7
  104.4 0.8 constant_dynamic-update-slice_fusion.6
  105.2 0.8 constant_dynamic-update-slice_fusion.5
  106.1 0.8 constant_dynamic-update-slice_fusion.4
  106.9 0.8 constant_dynamic-update-slice_fusion.3
  107.7 0.8 constant_dynamic-update-slice_fusion.2
  108.5 0.8 constant_dynamic-update-slice_fusion.1
  109.4 5.2 %broadcast_select_fusion = bf16[1536,1536]{1,0:T(8,128)(2,1)S(1)} fusion(bf16[1536,1536]{1,0:T(8,128)(2,1)} %collective-permute-done.15, pred[]{:T(512)S(6)} %eq.38, bf16[3072,1536]{1,0:T(8,128)(2,1)} %param.9, s32[]{:T(128)S(6)} %select_n.153), kind=kLoop, calls=%fused_computation.6 | loop fusion | flops 2359296 | bytes 14155781 | tf_op jit(solution)/shard_map/jit(_where)/select_n | solution.py:118
  114.6 1.5 collective-permute-start.16
  116.1 0.8 constant_dynamic-update-slice_fusion
  117.0 28.4 %convolution_convert_fusion.lrp_ref = bf16[2560,3072]{1,0:T(8,128)(2,1)} fusion(bf16[2560,1536]{1,0:T(8,128)(2,1)} %constant_dynamic-update-slice_fusion, bf16[3072,1536]{1,0:T(8,128)(2,1)S(1)} %bitcast.19), kind=kOutput, calls=%fused_computation.1 | convolution fusion | flops 24167055360 | bytes 33030144 | tf_op jit(solution)/shard_map/dot_general | solution.py:129
  145.4 18.2 %convolution_convert_fusion.1.lrq_ref = bf16[2560,1536]{1,0:T(8,128)(2,1)} fusion(bf16[2560,1536]{1,0:T(8,128)(2,1)} %constant_dynamic-update-slice_fusion, bf16[1536,1536]{1,0:T(8,128)(2,1)S(1)} %broadcast_select_fusion, bf16[1536,1536]{1,0:T(8,128)(2,1)} %collective-permute-done.16, pred[]{:T(512)S(6)} %eq.37), kind=kOutput, calls=%fused_computation.2 | convolution fusion | flops 12085886976 | bytes 25165824 | tf_op jit(solution)/shard_map/dot_general | solution.py:130
  163.7 92.0 %shard_map.73 = bf16[2560,1536]{1,0:T(8,128)(2,1)} custom-call(f32[8]{0:T(128)} %gather_fusion, bf16[1536,3072]{1,0:T(8,128)(2,1)} %bitcast.20, bf16[2560,3072]{1,0:T(8,128)(2,1)} %convolution_convert_fusion.lrp_ref, bf16[2560,1536]{1,0:T(8,128)(2,1)} %convolution_convert_fusion.1.lrq_ref), custom_call_target="tpu_custom_call" | custom-call | flops 48318382080 | bytes 56623104 | tf_op jit(solution)/shard_map/pallas_call | solution.py:52
  255.7 14.9 %convolution_convert_fusion.2 = bf16[1536,1536]{1,0:T(8,128)(2,1)S(1)} fusion(bf16[2560,1536]{1,0:T(8,128)(2,1)S(1)} %bitcast.22, bf16[2560,1536]{1,0:T(8,128)(2,1)} %shard_map.73), kind=kOutput, calls=%fused_computation.3 | convolution fusion | flops 12081954816 | bytes 20447232 | tf_op jit(solution)/shard_map/dot_general | solution.py:133
  270.6 2.2 copy-done
  272.7 0.2 constant_dynamic-slice_fusion.3
  272.9 1.8 collective-permute-start.17
  274.7 4.3 %collective-permute-done.17 = bf16[768,1536]{1,0:T(8,128)(2,1)} collective-permute-done((bf16[768,1536]{1,0:T(8,128)(2,1)S(1)}, bf16[768,1536]{1,0:T(8,128)(2,1)}, u32[]{:S(2)}, u32[]{:S(2)}) %collective-permute-start.17) | collective-permute-done | bytes 2359328 | tf_op jit(solution)/shard_map/ppermute | solution.py:75
  279.0 3.0 add_convert_fusion
  282.0 0.1 constant_dynamic-slice_fusion.2
  282.1 2.1 collective-permute-start.18
  284.2 26.1 %collective-permute-done.18 = bf16[384,1536]{1,0:T(8,128)(2,1)} collective-permute-done((bf16[384,1536]{1,0:T(8,128)(2,1)S(1)}, bf16[384,1536]{1,0:T(8,128)(2,1)}, u32[]{:S(2)}, u32[]{:S(2)}) %collective-permute-start.18) | collective-permute-done | bytes 1179680 | tf_op jit(solution)/shard_map/ppermute | solution.py:75
  310.4 1.5 add_convert_fusion.1
  311.9 0.1 constant_dynamic-slice_fusion.1
  312.0 3.9 %collective-permute-start.19 = (bf16[192,1536]{1,0:T(8,128)(2,1)S(1)}, bf16[192,1536]{1,0:T(8,128)(2,1)S(1)}, u32[]{:S(2)}, u32[]{:S(2)}) collective-permute-start(bf16[192,1536]{1,0:T(8,128)(2,1)S(1)} %get-tuple-element.9), channel_id=1, source_target_pairs={{0,0},{1,16},{2,8},{3,24},{4,4},{5,20},{6,12},{7,28},{8,1},{9,17},... | collective-permute-start | bytes 1769480 | tf_op jit(solution)/shard_map/ppermute | solution.py:75
  315.9 2.4 collective-permute-start.20
  318.3 30.8 %collective-permute-done.19 = bf16[192,1536]{1,0:T(8,128)(2,1)S(1)} collective-permute-done((bf16[192,1536]{1,0:T(8,128)(2,1)S(1)}, bf16[192,1536]{1,0:T(8,128)(2,1)S(1)}, u32[]{:S(2)}, u32[]{:S(2)}) %collective-permute-start.19) | collective-permute-done | bytes 589856 | tf_op jit(solution)/shard_map/ppermute | solution.py:75
  349.1 6.4 %collective-permute-done.20 = bf16[192,1536]{1,0:T(8,128)(2,1)S(1)} collective-permute-done((bf16[192,1536]{1,0:T(8,128)(2,1)S(1)}, bf16[192,1536]{1,0:T(8,128)(2,1)S(1)}, u32[]{:S(2)}, u32[]{:S(2)}) %collective-permute-start.20) | collective-permute-done | bytes 589856 | tf_op jit(solution)/shard_map/ppermute | solution.py:75
  355.5 0.1 broadcast_select_fusion.2
  355.6 1.7 convert_bitcast_fusion
  (41 shorter events, 0.1 us)
Async XLA Ops:
  0.0 17.5 %copy-start.4 = (u32[32]{0:T(128)S(1)}, u32[32]{0:T(128)}, u32[]{:S(2)}) copy-start(u32[32]{0:T(128)} %constant.106) | copy-start | bytes 388
  0.0 8.4 %copy-start.3 = (s32[20]{0:T(128)S(1)}, s32[20]{0:T(128)}, u32[]{:S(2)}) copy-start(s32[20]{0:T(128)} %param.13) | copy-start | bytes 244
  0.0 9.7 %copy-start.2 = (bf16[1,1536,160]{1,2,0:T(8,128)(2,1)S(1)}, bf16[1,1536,160]{1,2,0:T(8,128)(2,1)}, u32[]{:S(2)}) copy-start(bf16[1,1536,160]{1,2,0:T(8,128)(2,1)} %param.7) | copy-start | bytes 1474564
  0.0 9.7 %copy-start.1 = (bf16[1,1536,160]{1,2,0:T(8,128)(2,1)S(1)}, bf16[1,1536,160]{1,2,0:T(8,128)(2,1)}, u32[]{:S(2)}) copy-start(bf16[1,1536,160]{1,2,0:T(8,128)(2,1)} %param.8) | copy-start | bytes 1474564
  4.9 104.5 %collective-permute-start.15 = (bf16[1536,1536]{1,0:T(8,128)(2,1)}, bf16[1536,1536]{1,0:T(8,128)(2,1)}, u32[]{:S(2)}, u32[]{:S(2)}) collective-permute-start(bf16[1536,1536]{1,0:T(8,128)(2,1)} %constant_dynamic-slice_fusion.4), channel_id=1, source_target_pairs={{0,2},{4,6},{9,11},{13,15},{18,16},{22,20},{27,25},{31,29}} | collective-permute-start | bytes 14155784 | tf_op jit(solution)/shard_map/ppermute | solution.py:75
  10.8 40.5 %collective-permute-start = (bf16[160,1536]{1,0:T(8,128)(2,1)S(1)}, bf16[160,1536]{1,0:T(8,128)(2,1)S(1)}, u32[]{:S(2)}, u32[]{:S(2)}) collective-permute-start(bf16[160,1536]{1,0:T(8,128)(2,1)S(1)} %get-tuple-element.6), channel_id=1, source_target_pairs={{0,1},{1,0},{2,3},{3,2},{4,5},{5,4},{6,7},{7,6},{8,9},{9,8},{10,11... | collective-permute-start | bytes 1474568 | tf_op jit(solution)/shard_map/ppermute | solution.py:75
  15.1 42.3 %collective-permute-start.1 = (bf16[160,1536]{1,0:T(8,128)(2,1)S(1)}, bf16[160,1536]{1,0:T(8,128)(2,1)S(1)}, u32[]{:S(2)}, u32[]{:S(2)}) collective-permute-start(bf16[160,1536]{1,0:T(8,128)(2,1)S(1)} %get-tuple-element.6), channel_id=1, source_target_pairs={{0,4},{4,0},{8,12},{12,8},{16,20},{20,16},{24,28},{28,24},{1,5},{5... | collective-permute-start | bytes 1474568 | tf_op jit(solution)/shard_map/ppermute | solution.py:75
  16.3 46.0 %collective-permute-start.3 = (bf16[160,1536]{1,0:T(8,128)(2,1)S(1)}, bf16[160,1536]{1,0:T(8,128)(2,1)S(1)}, u32[]{:S(2)}, u32[]{:S(2)}) collective-permute-start(bf16[160,1536]{1,0:T(8,128)(2,1)S(1)} %get-tuple-element.6), channel_id=1, source_target_pairs={{0,24},{4,28},{8,0},{12,4},{16,8},{20,12},{24,16},{28,20},{1,25},{... | collective-permute-start | bytes 1474568 | tf_op jit(solution)/shard_map/ppermute | solution.py:75
  18.8 58.6 %collective-permute-start.7 = (bf16[160,1536]{1,0:T(8,128)(2,1)S(1)}, bf16[160,1536]{1,0:T(8,128)(2,1)S(1)}, u32[]{:S(2)}, u32[]{:S(2)}) collective-permute-start(bf16[160,1536]{1,0:T(8,128)(2,1)S(1)} %get-tuple-element.6), channel_id=1, source_target_pairs={{0,16},{4,20},{8,24},{12,28},{16,0},{20,4},{24,8},{28,12},{1,17},{... | collective-permute-start | bytes 1474568 | tf_op jit(solution)/shard_map/ppermute | solution.py:75
  51.3 27.3 %collective-permute-start.11 = (bf16[160,1536]{1,0:T(8,128)(2,1)S(1)}, bf16[160,1536]{1,0:T(8,128)(2,1)S(1)}, u32[]{:S(2)}, u32[]{:S(2)}) collective-permute-start(bf16[160,1536]{1,0:T(8,128)(2,1)S(1)} %get-tuple-element.6), channel_id=1, source_target_pairs={{0,8},{4,12},{8,16},{12,20},{16,24},{20,28},{24,0},{28,4},{1,9},{5... | collective-permute-start | bytes 1474568 | tf_op jit(solution)/shard_map/ppermute | solution.py:75
  57.4 22.2 %collective-permute-start.2 = (bf16[160,1536]{1,0:T(8,128)(2,1)S(1)}, bf16[160,1536]{1,0:T(8,128)(2,1)}, u32[]{:S(2)}, u32[]{:S(2)}) collective-permute-start(bf16[160,1536]{1,0:T(8,128)(2,1)S(1)} %collective-permute-done.1), channel_id=1, source_target_pairs={{0,1},{1,0},{2,3},{3,2},{4,5},{5,4},{6,7},{7,6},{8,9},{9,8},{10,11... | collective-permute-start | bytes 1474568 | tf_op jit(solution)/shard_map/ppermute | solution.py:75
  62.2 17.9 %collective-permute-start.5 = (bf16[160,1536]{1,0:T(8,128)(2,1)S(1)}, bf16[160,1536]{1,0:T(8,128)(2,1)S(1)}, u32[]{:S(2)}, u32[]{:S(2)}) collective-permute-start(bf16[160,1536]{1,0:T(8,128)(2,1)S(1)} %collective-permute-done.3), channel_id=1, source_target_pairs={{0,4},{4,0},{8,12},{12,8},{16,20},{20,16},{24,28},{28,24},{1,5},{5... | collective-permute-start | bytes 1474568 | tf_op jit(solution)/shard_map/ppermute | solution.py:75
  77.5 6.1 %collective-permute-start.4 = (bf16[160,1536]{1,0:T(8,128)(2,1)S(1)}, bf16[160,1536]{1,0:T(8,128)(2,1)S(1)}, u32[]{:S(2)}, u32[]{:S(2)}) collective-permute-start(bf16[160,1536]{1,0:T(8,128)(2,1)S(1)} %collective-permute-done.3), channel_id=1, source_target_pairs={{0,1},{1,0},{2,3},{3,2},{4,5},{5,4},{6,7},{7,6},{8,9},{9,8},{10,11... | collective-permute-start | bytes 1474568 | tf_op jit(solution)/shard_map/ppermute | solution.py:75
  78.6 12.7 %collective-permute-start.9 = (bf16[160,1536]{1,0:T(8,128)(2,1)S(1)}, bf16[160,1536]{1,0:T(8,128)(2,1)S(1)}, u32[]{:S(2)}, u32[]{:S(2)}) collective-permute-start(bf16[160,1536]{1,0:T(8,128)(2,1)S(1)} %collective-permute-done.7), channel_id=1, source_target_pairs={{0,4},{4,0},{8,12},{12,8},{16,20},{20,16},{24,28},{28,24},{1,5},{5... | collective-permute-start | bytes 1474568 | tf_op jit(solution)/shard_map/ppermute | solution.py:75
  79.6 22.2 %collective-permute-start.13 = (bf16[160,1536]{1,0:T(8,128)(2,1)S(1)}, bf16[160,1536]{1,0:T(8,128)(2,1)S(1)}, u32[]{:S(2)}, u32[]{:S(2)}) collective-permute-start(bf16[160,1536]{1,0:T(8,128)(2,1)S(1)} %collective-permute-done.11), channel_id=1, source_target_pairs={{0,4},{4,0},{8,12},{12,8},{16,20},{20,16},{24,28},{28,24},{1,5},{5... | collective-permute-start | bytes 1474568 | tf_op jit(solution)/shard_map/ppermute | solution.py:75
  80.1 22.7 %collective-permute-start.6 = (bf16[160,1536]{1,0:T(8,128)(2,1)S(1)}, bf16[160,1536]{1,0:T(8,128)(2,1)S(1)}, u32[]{:S(2)}, u32[]{:S(2)}) collective-permute-start(bf16[160,1536]{1,0:T(8,128)(2,1)S(1)} %collective-permute-done.5), channel_id=1, source_target_pairs={{0,1},{1,0},{2,3},{3,2},{4,5},{5,4},{6,7},{7,6},{8,9},{9,8},{10,11... | collective-permute-start | bytes 1474568 | tf_op jit(solution)/shard_map/ppermute | solution.py:75
  83.5 20.9 %collective-permute-start.8 = (bf16[160,1536]{1,0:T(8,128)(2,1)S(1)}, bf16[160,1536]{1,0:T(8,128)(2,1)S(1)}, u32[]{:S(2)}, u32[]{:S(2)}) collective-permute-start(bf16[160,1536]{1,0:T(8,128)(2,1)S(1)} %collective-permute-done.7), channel_id=1, source_target_pairs={{0,1},{1,0},{2,3},{3,2},{4,5},{5,4},{6,7},{7,6},{8,9},{9,8},{10,11... | collective-permute-start | bytes 1474568 | tf_op jit(solution)/shard_map/ppermute | solution.py:75
  91.3 16.4 %collective-permute-start.12 = (bf16[160,1536]{1,0:T(8,128)(2,1)S(1)}, bf16[160,1536]{1,0:T(8,128)(2,1)S(1)}, u32[]{:S(2)}, u32[]{:S(2)}) collective-permute-start(bf16[160,1536]{1,0:T(8,128)(2,1)S(1)} %collective-permute-done.11), channel_id=1, source_target_pairs={{0,1},{1,0},{2,3},{3,2},{4,5},{5,4},{6,7},{7,6},{8,9},{9,8},{10,11... | collective-permute-start | bytes 1474568 | tf_op jit(solution)/shard_map/ppermute | solution.py:75
  101.8 4.2 %collective-permute-start.10 = (bf16[160,1536]{1,0:T(8,128)(2,1)S(1)}, bf16[160,1536]{1,0:T(8,128)(2,1)S(1)}, u32[]{:S(2)}, u32[]{:S(2)}) collective-permute-start(bf16[160,1536]{1,0:T(8,128)(2,1)S(1)} %collective-permute-done.9), channel_id=1, source_target_pairs={{0,1},{1,0},{2,3},{3,2},{4,5},{5,4},{6,7},{7,6},{8,9},{9,8},{10,11... | collective-permute-start | bytes 1474568 | tf_op jit(solution)/shard_map/ppermute | solution.py:75
  102.8 13.3 %collective-permute-start.14 = (bf16[160,1536]{1,0:T(8,128)(2,1)S(1)}, bf16[160,1536]{1,0:T(8,128)(2,1)S(1)}, u32[]{:S(2)}, u32[]{:S(2)}) collective-permute-start(bf16[160,1536]{1,0:T(8,128)(2,1)S(1)} %collective-permute-done.13), channel_id=1, source_target_pairs={{0,1},{1,0},{2,3},{3,2},{4,5},{5,4},{6,7},{7,6},{8,9},{9,8},{10,11... | collective-permute-start | bytes 1474568 | tf_op jit(solution)/shard_map/ppermute | solution.py:75
  107.7 9.2 %slice-start = ((s8[9437184]{0:T(1024)(128)(4,1)}), s8[4194304]{0:T(1024)(128)(4,1)S(1)}, s32[]{:S(2)}) async-start(s8[9437184]{0:T(1024)(128)(4,1)} %bitcast.18), calls=%async_computation | async-start | bytes 8388608
  109.4 7.6 %slice-start.1 = ((s8[9437184]{0:T(1024)(128)(4,1)}), s8[4194304]{0:T(1024)(128)(4,1)S(1)}, s32[]{:S(2)}) async-start(s8[9437184]{0:T(1024)(128)(4,1)} %bitcast.18), calls=%async_computation.1 | async-start | bytes 8388608
  109.4 7.6 %slice-start.2 = ((s8[9437184]{0:T(1024)(128)(4,1)}), s8[1048576]{0:T(1024)(128)(4,1)S(1)}, s32[]{:S(2)}) async-start(s8[9437184]{0:T(1024)(128)(4,1)} %bitcast.18), calls=%async_computation.2 | async-start | bytes 2097152
  114.6 30.8 %collective-permute-start.16 = (bf16[1536,1536]{1,0:T(8,128)(2,1)S(1)}, bf16[1536,1536]{1,0:T(8,128)(2,1)}, u32[]{:S(2)}, u32[]{:S(2)}) collective-permute-start(bf16[1536,1536]{1,0:T(8,128)(2,1)S(1)} %broadcast_select_fusion), channel_id=1, source_target_pairs={{0,1},{2,3},{4,5},{6,7},{9,8},{11,10},{13,12},{15,14},{18,19},{16,... | collective-permute-start | bytes 14155784 | tf_op jit(solution)/shard_map/ppermute | solution.py:75
  145.4 110.3 %slice-start.3 = ((s8[7864320]{0:T(1024)(128)(4,1)}), s8[3670016]{0:T(1024)(128)(4,1)S(1)}, s32[]{:S(2)}) async-start(s8[7864320]{0:T(1024)(128)(4,1)} %bitcast.21), calls=%async_computation.3 | async-start | bytes 7340032
  163.7 92.0 %slice-start.4 = ((s8[7864320]{0:T(1024)(128)(4,1)}), s8[4194304]{0:T(1024)(128)(4,1)S(1)}, s32[]{:S(2)}) async-start(s8[7864320]{0:T(1024)(128)(4,1)} %bitcast.21), calls=%async_computation.4 | async-start | bytes 8388608
  270.6 2.2 copy-start
  272.9 6.1 %collective-permute-start.17 = (bf16[768,1536]{1,0:T(8,128)(2,1)S(1)}, bf16[768,1536]{1,0:T(8,128)(2,1)}, u32[]{:S(2)}, u32[]{:S(2)}) collective-permute-start(bf16[768,1536]{1,0:T(8,128)(2,1)S(1)} %constant_dynamic-slice_fusion.3), channel_id=1, source_target_pairs={{0,1},{1,0},{2,3},{3,2},{4,5},{5,4},{6,7},{7,6},{8,9},{9,8},{10,11... | collective-permute-start | bytes 7077896 | tf_op jit(solution)/shard_map/ppermute | solution.py:75
  282.1 28.3 %collective-permute-start.18 = (bf16[384,1536]{1,0:T(8,128)(2,1)S(1)}, bf16[384,1536]{1,0:T(8,128)(2,1)}, u32[]{:S(2)}, u32[]{:S(2)}) collective-permute-start(bf16[384,1536]{1,0:T(8,128)(2,1)S(1)} %constant_dynamic-slice_fusion.2), channel_id=1, source_target_pairs={{0,2},{1,3},{2,0},{3,1},{4,6},{5,7},{6,4},{7,5},{8,10},{9,11},{10,... | collective-permute-start | bytes 3538952 | tf_op jit(solution)/shard_map/ppermute | solution.py:75
  312.0 37.1 %collective-permute-start.19 = (bf16[192,1536]{1,0:T(8,128)(2,1)S(1)}, bf16[192,1536]{1,0:T(8,128)(2,1)S(1)}, u32[]{:S(2)}, u32[]{:S(2)}) collective-permute-start(bf16[192,1536]{1,0:T(8,128)(2,1)S(1)} %get-tuple-element.9), channel_id=1, source_target_pairs={{0,0},{1,16},{2,8},{3,24},{4,4},{5,20},{6,12},{7,28},{8,1},{9,17},... | collective-permute-start | bytes 1769480 | tf_op jit(solution)/shard_map/ppermute | solution.py:75
  315.9 39.6 %collective-permute-start.20 = (bf16[192,1536]{1,0:T(8,128)(2,1)S(1)}, bf16[192,1536]{1,0:T(8,128)(2,1)S(1)}, u32[]{:S(2)}, u32[]{:S(2)}) collective-permute-start(bf16[192,1536]{1,0:T(8,128)(2,1)S(1)} %get-tuple-element.10), channel_id=1, source_target_pairs={{0,4},{1,20},{2,12},{3,28},{4,0},{5,16},{6,8},{7,24},{8,5},{9,21},... | collective-permute-start | bytes 1769480 | tf_op jit(solution)/shard_map/ppermute | solution.py:75
